TPU v7x, 512 devices: a whole 4x8x8 slice. The times are simulated.
512 devices in a mesh: groups: 64 (over z_hi, y, core), tensor: 8 (over x, z_lo).
Axes of the slice: x: 4, y: 8, z: 8 (z_hi: 4, z_lo: 2; z = z_hi * 2 + z_lo), core: 2. Of those that a mesh axis runs over, the one named last changes fastest.
Arguments:
- tokens_old: bfloat16 [256, 8192], P('groups', 'tensor'), may hold values from -32 to 32
- tokens_new: bfloat16 [256, 8192], P('groups', 'tensor'), may hold values from -32 to 32
- norm_gain: float32 [8192], P('tensor'), may hold values from 0.1 to 1.9
- gate_base: bfloat16 [8192, 28672], P('tensor', 'groups'), may hold values from -0.0625 to 0.0625
- up_base: bfloat16 [8192, 28672], P('tensor', 'groups'), may hold values from -0.0625 to 0.0625
- down_base: bfloat16 [28672, 8192], P('groups', 'tensor'), may hold values from -0.03125 to 0.03125
- gate_left: bfloat16 [8192, 64], P(('tensor', 'groups')), may hold values from -0.0625 to 0.0625
- gate_right: bfloat16 [64, 28672], P(None, 'groups'), may hold values from -0.75 to 0.75
- up_left: bfloat16 [8192, 64], P(('tensor', 'groups')), may hold values from -0.0625 to 0.0625
- up_right: bfloat16 [64, 28672], P(None, 'groups'), may hold values from -0.75 to 0.75
- down_left: bfloat16 [28672, 64], P('groups'), may hold values from -0.03125 to 0.03125
- down_right: bfloat16 [8192, 64], P(('tensor', 'groups')), may hold values from -0.75 to 0.75
Outputs:
- out_old: bfloat16 [256, 8192], P('groups', 'tensor')
- out_new: bfloat16 [256, 8192], P('groups', 'tensor')
All inputs are finite; a program needn't handle non-finite values.
Results may differ from a plain program's by a relative error of at most 0.0082.
Values may be sent and summed in bfloat16 or wider, within the bound.
A program may use at most 64 MiB of HBM per device.

v0:
```python
import jax
import jax.numpy as jnp
from jax import lax
from jax.sharding import PartitionSpec as P

D = 8192
R = 64
ALPHA = 32


def merge_shard(base_shard, product):
    return (base_shard.astype(jnp.float32) + ALPHA / R * product).astype(jnp.bfloat16)


def decode(tokens, norm_gain, gate_weight, up_weight, down_weight):
    values = tokens.astype(jnp.float32)
    square_part = jnp.sum(values * values, axis=1)
    scaled = (values * norm_gain).astype(jnp.bfloat16)
    gate_part = jnp.dot(scaled, gate_weight, preferred_element_type=jnp.float32)
    up_part = jnp.dot(scaled, up_weight, preferred_element_type=jnp.float32)
    gate_sum, up_sum, square_sum = lax.psum((gate_part, up_part, square_part), "tensor")
    inverse = lax.rsqrt(square_sum / D + 1e-05)[:, None]
    hidden = (jax.nn.silu(gate_sum * inverse) * (up_sum * inverse)).astype(jnp.bfloat16)
    return lax.psum_scatter(
        jnp.dot(hidden, down_weight, preferred_element_type=jnp.float32),
        "groups",
        scatter_dimension=0,
        tiled=True,
    ).astype(jnp.bfloat16)


def per_device(
    tokens_old,
    tokens_new,
    norm_gain,
    gate_base,
    up_base,
    down_base,
    gate_left,
    gate_right,
    up_left,
    up_right,
    down_left,
    down_right,
):
    rows_old, rows_new = (
        lax.all_gather(tokens_old, "groups", axis=0, tiled=True),
        lax.all_gather(tokens_new, "groups", axis=0, tiled=True),
    )
    gate_full, up_full, down_full = (
        lax.all_gather(gate_left, "groups", axis=0, tiled=True),
        lax.all_gather(up_left, "groups", axis=0, tiled=True),
        lax.all_gather(down_right, "groups", axis=0, tiled=True),
    )
    out_old = decode(rows_old, norm_gain, gate_base, up_base, down_base)
    gate_merged = merge_shard(
        gate_base, jnp.dot(gate_full, gate_right, preferred_element_type=jnp.float32)
    )
    up_merged = merge_shard(up_base, jnp.dot(up_full, up_right, preferred_element_type=jnp.float32))
    down_product = lax.dot_general(
        down_left, down_full, (((1,), (1,)), ((), ())), preferred_element_type=jnp.float32
    )
    down_merged = merge_shard(down_base, down_product)
    out_new = decode(rows_new, norm_gain, gate_merged, up_merged, down_merged)
    return (out_old, out_new)


def solution(mesh):
    in_specs = (
        P("groups", "tensor"),
        P("groups", "tensor"),
        P("tensor"),
        P("tensor", "groups"),
        P("tensor", "groups"),
        P("groups", "tensor"),
        P(("tensor", "groups"), None),
        P(None, "groups"),
        P(("tensor", "groups"), None),
        P(None, "groups"),
        P("groups", None),
        P(("tensor", "groups"), None),
    )
    out_specs = (P("groups", "tensor"), P("groups", "tensor"))
    return jax.shard_map(
        per_device, mesh=mesh, in_specs=in_specs, out_specs=out_specs, check_vma=False
    )
```

profile of v0, /device:TPU:6, one launch (start us, length us, event | category | flops | bytes accessed | tf_op | source)
XLA Modules:
  0.0 763.0 jit_solution(12249250251614621579)
XLA Ops:
  7.2 0.0 copy-start
  7.2 0.0 all-reduce.8.cloned.1.call-start
  7.2 0.0 copy-start.5
  7.2 90.2 %all-gather.1 = bf16[64,4,1024]{2,1,0:T(4,128)(2,1)S(1)} all-gather(bf16[1,4,1024]{2,1,0:T(4,128)(2,1)} %bitcast.12), channel_id=1, replica_groups=mesh['groups'=64,'tensor'=8] {'groups'}, dimensions={0}, use_global_device_ids=true | all-gather | bytes 532480 | tf_op jit(solution)/shard_map/all_gather | solution.py:48
  97.5 0.1 reshape.12
  97.5 0.0 copy-done.5
  97.5 0.0 copy-start.6
  97.6 77.9 %all-gather = bf16[64,4,1024]{2,1,0:T(4,128)(2,1)S(1)} all-gather(bf16[1,4,1024]{2,1,0:T(4,128)(2,1)S(1)} %bitcast.13), channel_id=1, replica_groups=mesh['groups'=64,'tensor'=8] {'groups'}, dimensions={0}, use_global_device_ids=true | all-gather | bytes 532480 | tf_op jit(solution)/shard_map/all_gather | solution.py:47
  175.5 0.0 copy-start.7
  175.5 0.0 copy-start.2
  175.5 0.1 reshape.11
  175.5 0.0 copy-done.6
  175.6 83.7 %all_gather.17 = bf16[1024,64]{1,0:T(8,128)(2,1)} all-gather(bf16[16,64]{1,0:T(8,128)(2,1)S(1)} %copy-done.6), channel_id=1, replica_groups=mesh['groups'=64,'tensor'=8] {'groups'}, dimensions={0}, use_global_device_ids=true | all-gather | bytes 133120 | tf_op jit(solution)/shard_map/all_gather | solution.py:51
  259.3 0.0 copy-done.7
  259.3 77.2 %all_gather.18 = bf16[1024,64]{1,0:T(8,128)(2,1)S(1)} all-gather(bf16[16,64]{1,0:T(8,128)(2,1)S(1)} %copy-done.7), channel_id=1, replica_groups=mesh['groups'=64,'tensor'=8] {'groups'}, dimensions={0}, use_global_device_ids=true | all-gather | bytes 133120 | tf_op jit(solution)/shard_map/all_gather | solution.py:52
  336.5 0.0 copy-done.2
  336.5 0.0 copy-start.1
  336.5 2.5 fusion.11
  339.0 0.0 copy-done.1
  339.0 0.0 copy-start.3
  339.0 1.2 fusion.12
  340.2 0.0 copy-done.3
  340.2 0.0 copy-start.4
  340.2 2.6 fusion
  342.8 0.0 copy-done.4
  342.8 2.8 fusion.1
  345.5 0.0 all-reduce.8.cloned.1.call-update
  345.6 1.3 dynamic-slice
  347.5 0.0 copy-start.8
  347.5 0.0 copy-start.9
  347.5 0.1 multiply_reduce_fusion
  347.7 0.1 multiply_reduce_fusion.1
  347.8 17.1 %all-reduce.3 = (f32[256]{0:T(256)S(1)}, f32[256]{0:T(256)S(1)}) all-reduce(f32[256]{0:T(256)S(1)} %multiply_reduce_fusion.1, f32[256]{0:T(256)S(1)} %multiply_reduce_fusion), channel_id=1, replica_groups=mesh['groups'=64,'tensor'=8] {'tensor'}, use_global_device_ids=true, to_apply=%region_2.0 | all-reduce | flops 512 | bytes 4096 | tf_op jit(solution)/shard_map/psum | solution.py:21
  364.9 0.0 copy-done.8
  364.9 79.3 %all_gather.19 = bf16[1024,64]{1,0:T(8,128)(2,1)S(1)} all-gather(bf16[16,64]{1,0:T(8,128)(2,1)S(1)} %copy-done.8), channel_id=1, replica_groups=mesh['groups'=64,'tensor'=8] {'groups'}, dimensions={0}, use_global_device_ids=true | all-gather | bytes 133120 | tf_op jit(solution)/shard_map/all_gather | solution.py:53
  444.3 0.4 all-reduce.8.cloned.1.call-done
  444.6 0.0 copy-done
  444.6 0.0 copy-done.9
  444.6 0.0 copy-start.10
  444.6 2.0 fusion.2
  446.7 0.0 copy-done.10
  446.7 1.6 fusion.6
  448.2 306.6 %all-reduce.9 = (bf16[256,1024]{1,0:T(8,128)(2,1)S(1)}, bf16[256,1024]{1,0:T(8,128)(2,1)S(1)}) all-reduce(f32[256,1024]{1,0:T(8,128)S(1)} %fusion.6, f32[256,1024]{1,0:T(8,128)S(1)} %fusion.2), channel_id=2, replica_groups=mesh['groups'=64,'tensor'=8] {'groups'}, use_global_device_ids=true, to_apply=%region_4.5.clone | all-reduce | flops 524288 | bytes 3145728
  754.9 0.6 dynamic-slice_convert_fusion
  755.5 0.6 dynamic-slice_convert_fusion.1
  (1 shorter events, 0.0 us)
Async XLA Ops:
  7.2 437.5 %copy-start = (bf16[448,64]{0,1:T(8,128)(2,1)S(1)}, bf16[448,64]{0,1:T(8,128)(2,1)}, u32[]{:S(2)}) copy-start(bf16[448,64]{0,1:T(8,128)(2,1)} %param.22) | copy-start | bytes 172036
  7.2 437.4 %all-reduce.8.cloned.1.call-start = ((), (), s32[]{:S(2)}) async-start(), calls=%async_computation | async-start | bytes 3670016 | tf_op jit(solution)/shard_map/psum | solution.py:21
  7.2 90.3 %copy-start.5 = (bf16[4,1024]{1,0:T(4,128)(2,1)S(1)}, bf16[4,1024]{1,0:T(4,128)(2,1)}, u32[]{:S(2)}) copy-start(bf16[4,1024]{1,0:T(4,128)(2,1)} %param.12) | copy-start | bytes 24580
  97.5 78.0 %copy-start.6 = (bf16[16,64]{1,0:T(8,128)(2,1)S(1)}, bf16[16,64]{1,0:T(8,128)(2,1)}, u32[]{:S(2)}) copy-start(bf16[16,64]{1,0:T(8,128)(2,1)} %param.18) | copy-start | bytes 6148
  175.5 83.8 %copy-start.7 = (bf16[16,64]{1,0:T(8,128)(2,1)S(1)}, bf16[16,64]{1,0:T(8,128)(2,1)}, u32[]{:S(2)}) copy-start(bf16[16,64]{1,0:T(8,128)(2,1)} %param.20) | copy-start | bytes 6148
  175.5 161.0 %copy-start.2 = (f32[1024]{0:T(1024)S(1)}, f32[1024]{0:T(1024)}, u32[]{:S(2)}) copy-start(f32[1024]{0:T(1024)} %param.14) | copy-start | bytes 12292
  336.5 2.5 copy-start.1
  339.0 1.2 copy-start.3
  340.2 2.6 copy-start.4
  347.5 17.5 %copy-start.8 = (bf16[16,64]{1,0:T(8,128)(2,1)S(1)}, bf16[16,64]{1,0:T(8,128)(2,1)}, u32[]{:S(2)}) copy-start(bf16[16,64]{1,0:T(8,128)(2,1)} %param.23) | copy-start | bytes 6148
  347.5 97.1 %copy-start.9 = (bf16[448,1024]{1,0:T(8,128)(2,1)S(1)}, bf16[448,1024]{1,0:T(8,128)(2,1)}, u32[]{:S(2)}) copy-start(bf16[448,1024]{1,0:T(8,128)(2,1)} %param.17) | copy-start | bytes 2752516
  444.6 2.0 copy-start.10
Sparse Core Ops, SparseCore 0:
  345.7 98.8 all-reduce.7
where the time goes:
time: 768 us; the launch traced here: 763 us
  blocking collectives  732 us (95%)
  between operations  14.8 us (2%)
  matrix products  12.6 us (2%)
    unnamed x1, blocking collectives  307 us
    all_gather x1, blocking collectives, per_device(): lax.all_gather(tokens_new, 'groups', axis=0, tiled=True)  90.2 us
    all_gather x1, blocking collectives, per_device(): lax.all_gather(gate_left, 'groups', axis=0, tiled=True)  83.7 us
    all_gather x1, blocking collectives, per_device(): lax.all_gather(down_right, 'groups', axis=0, tiled=True)  79.3 us
    all_gather x1, blocking collectives, per_device(): lax.all_gather(tokens_old, 'groups', axis=0, tiled=True)  77.9 us
    all_gather x1, blocking collectives, per_device(): lax.all_gather(up_left, 'groups', axis=0, tiled=True)  77.2 us
    psum x1, blocking collectives, decode(): lax.psum((gate_part, up_part, square_part), 'tensor')  17.1 us
  transfers between devices with their start and end apart: 1, of which 1 were waited for; matrix products, arithmetic and copies ran while one was open for 0% of the time, Pallas kernels for 0%

commit v1 on v0

v1 whole, which is shorter than its diff:
```python
import functools

import jax
import jax.numpy as jnp
from jax import lax
from jax.experimental import pallas as pl
from jax.experimental.pallas import tpu as pltpu
from jax.sharding import PartitionSpec as P

MESH = pl.DeviceIdType.MESH
F32, BF16 = jnp.float32, jnp.bfloat16
D = 8192
R = 64
ALPHA = 32
NZ, NY, NT = 4, 8, 8
DL, FL = 1024, 448
ROWS, OWN = 256, 4
HALF = ROWS // 2
BLOCK = ROWS // NT
LANES = 128
CHUNKS = DL // LANES
Z_ORDER = (2, 1, 3)
Y_ORDER = (4, 3, 5, 2, 6, 1, 7)


def block_target(b):
    x = b % 4
    return x * 2 + (b // 4 + x) % 2


def fold(values):
    return [values[:, j * LANES : (j + 1) * LANES] for j in range(CHUNKS)]


def kernel(
    old_ref, new_ref, gain_ref, gl_ref, ul_ref, dr_ref, gr_ref, ur_ref, dl_ref, gate_hbm, up_hbm, down_hbm,
    out_old_ref, out_new_ref,
    gate_v, up_v, down_v, w_old, w_new, down_new, rcomb,
    s1_old, s1_new, fac, x_old, x_new,
    p_old, p_new, t_old, t_new, h_old, h_new,
    d_own, d_sib_old, d_sib_new, e_old, e_new, cs_old, cs_new, r1_old, r1_new, c2_old, c2_new, r2_old, r2_new, inv_new,
    local_sem, ss, rs,
):
    g, t = lax.axis_index("groups"), lax.axis_index("tensor")
    zh, y, c = g // 16, (g // 2) % 8, g % 2
    pos = (t // 2) + 4 * ((t % 2 + t // 2) % 2)
    sibling = (zh * 16 + y * 2 + (1 - c), t)

    def z_peer(k):
        return (((zh + k) % NZ) * 16 + y * 2 + c, t)

    def y_peer(k):
        return (zh * 16 + ((y + k) % NY) * 2 + c, t)

    counter = [0]
    pending = {0: [], 1: [], None: []}

    def sems(n):
        counter[0] += n
        return counter[0] - n

    def remote(src, dst, s, r, dev):
        return pltpu.make_async_remote_copy(
            src_ref=src, dst_ref=dst, send_sem=ss.at[s], recv_sem=rs.at[r], device_id=dev, device_id_type=MESH
        )

    loads = [
        pltpu.make_async_copy(gate_hbm, gate_v, local_sem.at[0]),
        pltpu.make_async_copy(up_hbm, up_v, local_sem.at[1]),
        pltpu.make_async_copy(down_hbm, down_v, local_sem.at[2]),
    ]
    for load in loads:
        load.start()

    barrier = pltpu.get_barrier_semaphore()
    greet = [sibling] + [z_peer(k) for k in Z_ORDER] + [y_peer(k) for k in Y_ORDER]
    greet += [(g, (t + k) % NT) for k in range(1, NT)]
    for dev in greet:
        pl.semaphore_signal(barrier, inc=1, device_id=dev, device_id_type=MESH)

    lane = lax.broadcasted_iota(jnp.int32, (OWN, LANES), 1)
    sums = jnp.zeros((OWN, LANES), F32)
    gain = gain_ref[...]
    folded = []
    for i, ref in enumerate((old_ref, new_ref)):
        values = ref[...].astype(F32)
        square = jnp.sum(values * values, axis=1, keepdims=True)
        high = square.astype(BF16).astype(F32)
        sums = jnp.where(lane == 2 * i, high, sums)
        sums = jnp.where(lane == 2 * i + 1, square - high, sums)
        folded.append(fold(values * gain))
    zeros = jnp.zeros((48 - CHUNKS * OWN - OWN, LANES), F32)
    s1_old[0] = jnp.concatenate(folded[0] + [sums, zeros], axis=0).astype(BF16)
    s1_new[0] = jnp.concatenate(folded[1], axis=0).astype(BF16)
    left = jnp.concatenate([gl_ref[...], ul_ref[...]], axis=1)
    right = jnp.concatenate([dr_ref[...], jnp.zeros((16, LANES - R), BF16)], axis=1)
    fac[c, y, zh] = jnp.concatenate([left, right], axis=0)

    pl.semaphore_wait(barrier, len(greet))

    class Plane:
        def __init__(self, core):
            self.core = core
            first = (NZ, Z_ORDER, z_peer)
            second = (NY, Y_ORDER, y_peer)
            if core == 1:
                first, second = second, first
            self.n1, self.order1, self.peer1 = first
            self.n2, self.order2, self.peer2 = second
            self.rows = OWN * self.n1

        def block(self, k):
            return pl.ds(k * self.rows, self.rows)

        def record(self, copies):
            pending[self.core] += copies
            return copies

    planes = (Plane(0), Plane(1))
    base = {}
    for name in ("a1o", "a1n", "a1f", "a2o", "a2n", "a2f", "fo", "fn", "c1o", "c1n", "c2o", "c2n", "to", "tn", "ho", "hn"):
        base[name] = sems(8)
    for name in ("ff", "eo", "en"):
        base[name] = sems(1)

    def stage1(pln, name, src, dst_of):
        return [remote(src, dst_of(k), base[name] + k, base[name] + k, pln.peer1(k)) for k in pln.order1]

    def a1_copies(pln):
        return (
            [remote(s1_old.at[0], s1_old.at[k], base["a1o"] + k, base["a1o"] + k, pln.peer1(k)) for k in pln.order1],
            [remote(s1_new.at[0], s1_new.at[k], base["a1n"] + k, base["a1n"] + k, pln.peer1(k)) for k in pln.order1],
            [
                remote(fac.at[c, y, zh], fac.at[c, y, zh], base["a1f"] + k, base["a1f"] + k, pln.peer1(k))
                for k in pln.order1
            ],
        )

    def a2_copies(pln, name, x_ref):
        return [
            remote(x_ref.at[0, pln.block(0)], x_ref.at[0, pln.block(k)], base[name] + k, base[name] + k, pln.peer2(k))
            for k in pln.order2
        ]

    def a2_factor_copies(pln):
        part = fac.at[c, y] if pln.core == 0 else fac.at[c, :, zh]
        return [remote(part, part, base["a2f"] + k, base["a2f"] + k, pln.peer2(k)) for k in pln.order2]

    def forward(pln, name, x_ref, k):
        return remote(x_ref.at[0, pln.block(k)], x_ref.at[1, pln.block(k)], base[name] + k, base[name], sibling)

    def assemble(pln, s1, x_ref, chunks):
        parts = [s1[k].astype(F32) for k in range(pln.n1)]
        for j in range(chunks):
            tile = jnp.concatenate([part[OWN * j : OWN * (j + 1)] for part in parts], axis=0)
            x_ref[0, 0 : pln.rows, j * LANES : (j + 1) * LANES] = tile.astype(BF16)

    def per_core(fn):
        for pln in planes:
            pl.when(c == pln.core)(functools.partial(fn, pln))

    def gather_first(pln):
        olds, news, facs = a1_copies(pln)
        for copy in olds + news + facs:
            copy.start()
        for copy in olds:
            copy.wait_recv()
        assemble(pln, s1_old, x_old, CHUNKS + 1)
        for copy in a2_copies(pln, "a2o", x_old):
            copy.start()
        forward(pln, "fo", x_old, 0).start()
        for copy in news:
            copy.wait_recv()
        assemble(pln, s1_new, x_new, CHUNKS)
        for copy in a2_copies(pln, "a2n", x_new):
            copy.start()
        forward(pln, "fn", x_new, 0).start()
        for copy in facs:
            copy.wait_recv()
        for copy in a2_factor_copies(pln):
            copy.start()

    per_core(gather_first)

    loads[0].wait()
    loads[1].wait()

    def join(i, carry):
        part = pl.ds(i * 128, 128)
        w_old[part, :] = jnp.concatenate([gate_v[part, :], up_v[part, :]], axis=1)
        return carry

    lax.fori_loop(0, DL // 128, join, 0)
    none = jnp.zeros((R, FL), BF16)
    rcomb[0:R, :] = jnp.concatenate([gr_ref[...], none], axis=1)
    rcomb[R : 2 * R, :] = jnp.concatenate([none, ur_ref[...]], axis=1)

    def gather_second(pln, name, forward_name, x_ref):
        copies = a2_copies(pln, name, x_ref)
        for k, copy in reversed(list(zip(pln.order2, copies))):
            copy.wait_recv()
            forward(pln, forward_name, x_ref, k).start()

    def wait_sibling_half(name, x_ref):
        remote(x_ref.at[0], x_ref.at[1], base[name], base[name], sibling).wait_recv()

    def reduce_copy(name, p_ref, t_ref, b):
        return remote(p_ref.at[b], t_ref.at[pos], base[name] + b, base[name] + pos, (g, block_target(b)))

    def project(half, x_ref, w_ref, p_ref, t_ref, name, with_sums):
        product = jnp.dot(x_ref[half, :, 0:DL], w_ref[...], preferred_element_type=F32)
        p_ref[4 * half : 4 * half + 4, :, 0 : 2 * FL] = product.astype(BF16).reshape(4, BLOCK, 2 * FL)
        if with_sums:
            p_ref[4 * half : 4 * half + 4, :, 2 * FL :] = x_ref[half, :, DL:].reshape(4, BLOCK, LANES)
        for b in range(4 * half, 4 * half + 4):
            pl.when(b != pos)(lambda b=b: reduce_copy(name, p_ref, t_ref, b).start())

    def reduced(p_ref, t_ref, name):
        t_ref[pos] = p_ref[pos]
        for b in range(NT):
            def wait(b=b):
                remote(p_ref.at[b], t_ref.at[b], base[name] + b, base[name] + b, (g, block_target(b))).wait_recv()
            pl.when(b != pos)(wait)
        total = t_ref[0].astype(F32)
        for b in range(1, NT):
            total += t_ref[b].astype(F32)
        return total

    def hidden_copies(name, h_ref):
        copies = []
        for k in (6, 2, 5, 3, 7, 1, 4):
            b = (pos + k) % NT
            copies.append(remote(h_ref.at[pos], h_ref.at[pos], base[name] + b, base[name] + pos, (g, block_target(b))))
        return copies

    def activate(total, inverse, name, h_ref):
        gate = total[:, 0:FL] * inverse
        up = total[:, FL : 2 * FL] * inverse
        h_ref[pos] = (gate / (1.0 + jnp.exp(-gate)) * up).astype(BF16)
        for copy in hidden_copies(name, h_ref):
            copy.start()

    def wait_hidden(name, h_ref, half):
        for b in range(4 * half, 4 * half + 4):
            def wait(b=b):
                remote(h_ref.at[b], h_ref.at[b], base[name] + b, base[name] + b, (g, block_target(b))).wait_recv()
            pl.when(b != pos)(wait)

    def down_project(h_name, h_ref, down_ref, d_sib, e_ref, e_name, cs_ref):
        wait_hidden(h_name, h_ref, 1)
        d_sib[...] = jnp.dot(
            h_ref[4:8].reshape(HALF, FL), down_ref[...], preferred_element_type=F32
        ).astype(BF16)
        exchange = remote(d_sib, e_ref, base[e_name], base[e_name], sibling)
        exchange.start()
        wait_hidden(h_name, h_ref, 0)
        d_own[...] = jnp.dot(h_ref[0:4].reshape(HALF, FL), down_ref[...], preferred_element_type=F32)
        exchange.wait_recv()
        d_own[...] += e_ref[...].astype(F32)
        cs_ref[...] = d_own[...].astype(BF16)

    def c1_copies(pln, name, cs_ref, r1_ref):
        return [
            remote(cs_ref.at[pln.block(k)], r1_ref.at[pln.block(k)], base[name] + k, base[name] + k, pln.peer2(-k))
            for k in pln.order2
        ]

    def c2_copies(pln, name, c2_ref, r2_ref):
        return [
            remote(c2_ref.at[k], r2_ref.at[k], base[name] + k, base[name] + k, pln.peer1(-k)) for k in pln.order1
        ]

    def scatter_first(pln, name, cs_ref, r1_ref):
        for copy in c1_copies(pln, name, cs_ref, r1_ref):
            copy.start()

    def scatter_second(pln, name1, cs_ref, r1_ref, name2, c2_ref, r2_ref):
        for copy in c1_copies(pln, name1, cs_ref, r1_ref):
            copy.wait_recv()
        total = cs_ref[pln.block(0)].astype(F32)
        for k in range(1, pln.n2):
            total += r1_ref[pln.block(k)].astype(F32)
        for k in range(pln.n1):
            piece = jnp.concatenate(fold(total[OWN * k : OWN * (k + 1)]), axis=0)
            c2_ref[k] = piece.astype(BF16)
        for copy in c2_copies(pln, name2, c2_ref, r2_ref):
            copy.start()

    def scatter_last(pln, name2, c2_ref, r2_ref, out_ref):
        for copy in c2_copies(pln, name2, c2_ref, r2_ref):
            copy.wait_recv()
        total = c2_ref[0].astype(F32)
        for k in range(1, pln.n1):
            total += r2_ref[k].astype(F32)
        out_ref[...] = jnp.concatenate(
            [total[OWN * j : OWN * (j + 1)] for j in range(CHUNKS)], axis=1
        ).astype(BF16)

    per_core(lambda pln: gather_second(pln, "a2o", "fo", x_old))
    project(0, x_old, w_old, p_old, t_old, "to", True)
    wait_sibling_half("fo", x_old)
    project(1, x_old, w_old, p_old, t_old, "to", True)

    per_core(lambda pln: gather_second(pln, "a2n", "fn", x_new))

    def gather_factors(pln):
        for copy in a2_factor_copies(pln):
            copy.wait_recv()

    per_core(gather_factors)
    plane = fac.at[c]
    factor_exchange = remote(plane, plane, base["ff"], base["ff"], sibling)
    factor_exchange.start()
    factor_exchange.wait_recv()
    loads[2].wait()

    def merge_in(q):
        rows = pl.ds(q * 256, 256)
        left = jnp.concatenate([fac[i % 2, i // 2, q, 0:16, :] for i in range(16)], axis=0)
        product = jnp.dot(left, rcomb[...], preferred_element_type=F32)
        w_new[rows, :] = (w_old[rows, :].astype(F32) + ALPHA / R * product).astype(BF16)

    def merge_down(q):
        columns = pl.ds(q * 256, 256)
        right = jnp.concatenate([fac[i % 2, i // 2, q, 16:32, 0:R] for i in range(16)], axis=0)
        product = lax.dot_general(dl_ref[...], right, (((1,), (1,)), ((), ())), preferred_element_type=F32)
        down_new[:, columns] = (down_v[:, columns].astype(F32) + ALPHA / R * product).astype(BF16)

    for q in range(4):
        merge_in(q)
    project(0, x_new, w_new, p_new, t_new, "tn", False)
    wait_sibling_half("fn", x_new)
    project(1, x_new, w_new, p_new, t_new, "tn", False)

    total = reduced(p_old, t_old, "to")
    mean = total[:, 2 * FL :] * (1.0 / D)
    inverse_old = lax.rsqrt(mean[:, 0:1] + mean[:, 1:2] + 1e-05)
    inv_new[...] = jnp.broadcast_to(lax.rsqrt(mean[:, 2:3] + mean[:, 3:4] + 1e-05), (BLOCK, LANES))
    activate(total, inverse_old, "ho", h_old)
    for q in range(4):
        merge_down(q)
    down_project("ho", h_old, down_v, d_sib_old, e_old, "eo", cs_old)
    per_core(lambda pln: scatter_first(pln, "c1o", cs_old, r1_old))

    total = reduced(p_new, t_new, "tn")
    activate(total, inv_new[:, 0:1], "hn", h_new)
    per_core(lambda pln: scatter_second(pln, "c1o", cs_old, r1_old, "c2o", c2_old, r2_old))
    down_project("hn", h_new, down_new, d_sib_new, e_new, "en", cs_new)
    per_core(lambda pln: scatter_first(pln, "c1n", cs_new, r1_new))
    per_core(lambda pln: scatter_last(pln, "c2o", c2_old, r2_old, out_old_ref))
    per_core(lambda pln: scatter_second(pln, "c1n", cs_new, r1_new, "c2n", c2_new, r2_new))
    per_core(lambda pln: scatter_last(pln, "c2n", c2_new, r2_new, out_new_ref))

    def drain(pln):
        for group in a1_copies(pln):
            for copy in group:
                copy.wait_send()
        copies = a2_copies(pln, "a2o", x_old) + a2_copies(pln, "a2n", x_new) + a2_factor_copies(pln)
        copies += [forward(pln, "fo", x_old, k) for k in range(pln.n2)]
        copies += [forward(pln, "fn", x_new, k) for k in range(pln.n2)]
        copies += c1_copies(pln, "c1o", cs_old, r1_old) + c1_copies(pln, "c1n", cs_new, r1_new)
        copies += c2_copies(pln, "c2o", c2_old, r2_old) + c2_copies(pln, "c2n", c2_new, r2_new)
        for copy in copies:
            copy.wait_send()

    per_core(drain)
    factor_exchange.wait_send()
    remote(d_sib_old, e_old, base["eo"], base["eo"], sibling).wait_send()
    remote(d_sib_new, e_new, base["en"], base["en"], sibling).wait_send()
    for b in range(NT):
        def wait(b=b):
            reduce_copy("to", p_old, t_old, b).wait_send()
            reduce_copy("tn", p_new, t_new, b).wait_send()
        pl.when(b != pos)(wait)
    for copy in hidden_copies("ho", h_old) + hidden_copies("hn", h_new):
        copy.wait_send()


def per_device(old, new, gain, gate, up, down, gl, gr, ul, ur, dl, dr):
    vmem = pl.BlockSpec(memory_space=pltpu.VMEM)
    hbm = pl.BlockSpec(memory_space=pl.ANY)
    scratch = [
        ((DL, FL), BF16), ((DL, FL), BF16), ((FL, DL), BF16),
        ((DL, 2 * FL), BF16), ((DL, 2 * FL), BF16), ((FL, DL), BF16), ((2 * R, 2 * FL), BF16),
        ((8, 48, LANES), BF16), ((8, 32, LANES), BF16), ((2, NY, NZ, 32, LANES), BF16),
        ((2, HALF, DL + LANES), BF16), ((2, HALF, DL), BF16),
        ((NT, BLOCK, 2 * FL + LANES), BF16), ((NT, BLOCK, 2 * FL), BF16),
        ((NT, BLOCK, 2 * FL + LANES), BF16), ((NT, BLOCK, 2 * FL), BF16),
        ((NT, BLOCK, FL), BF16), ((NT, BLOCK, FL), BF16),
        ((HALF, DL), F32), ((HALF, DL), BF16), ((HALF, DL), BF16),
        ((HALF, DL), BF16), ((HALF, DL), BF16), ((HALF, DL), BF16), ((HALF, DL), BF16),
        ((HALF, DL), BF16), ((HALF, DL), BF16),
        ((8, 32, LANES), BF16), ((8, 32, LANES), BF16), ((8, 32, LANES), BF16), ((8, 32, LANES), BF16),
        ((BLOCK, LANES), F32),
    ]
    flops = 2 * (2 * ROWS * DL * FL * 3 + 3 * DL * FL * R)
    return pl.pallas_call(
        kernel,
        out_shape=[jax.ShapeDtypeStruct((OWN, DL), BF16)] * 2,
        in_specs=[vmem] * 9 + [hbm] * 3,
        out_specs=[vmem, vmem],
        scratch_shapes=[pltpu.VMEM(shape, dtype) for shape, dtype in scratch]
        + [pltpu.SemaphoreType.DMA((3,)), pltpu.SemaphoreType.DMA((132,)), pltpu.SemaphoreType.DMA((132,))],
        compiler_params=pltpu.CompilerParams(
            collective_id=0, has_side_effects=True, vmem_limit_bytes=48 * 1024 * 1024
        ),
        cost_estimate=pl.CostEstimate(flops=flops, bytes_accessed=6 * DL * FL, transcendentals=2 * BLOCK * FL),
    )(old, new, gain.reshape(1, DL), gl, ul, dr, gr, ur, dl, gate, up, down)


def solution(mesh):
    in_specs = (
        P("groups", "tensor"),
        P("groups", "tensor"),
        P("tensor"),
        P("tensor", "groups"),
        P("tensor", "groups"),
        P("groups", "tensor"),
        P(("tensor", "groups"), None),
        P(None, "groups"),
        P(("tensor", "groups"), None),
        P(None, "groups"),
        P("groups", None),
        P(("tensor", "groups"), None),
    )
    out_specs = (P("groups", "tensor"), P("groups", "tensor"))
    return jax.shard_map(per_device, mesh=mesh, in_specs=in_specs, out_specs=out_specs, check_vma=False)
```

time: 768 us -> 73.3 us (0.10)
  blocking collectives: 732 us -> 0 us
  Pallas kernels: 0 us -> 66.6 us
  between operations: 14.8 us -> 0.8 us
  matrix products: 12.6 us -> 0 us
    all_gather x5 -> x0, blocking collectives: 408 us -> none  [the longest x1 90.2 us: per_device(): lax.all_gather(tokens_new, 'groups', axis=0, tiled=True)]
    unnamed x1 -> x0, blocking collectives: 307 us -> none
    pallas_call x0 -> x1, Pallas kernels: none -> 66.6 us  [per_device(): pl.pallas_call(kernel, out_shape=[jax.ShapeDtypeStruct((OWN, DL), BF16)]...]
    psum x1 -> x0, blocking collectives: 17.1 us -> none  [decode(): lax.psum((gate_part, up_part, square_part), 'tensor')]
    dot_general x6 -> x0, matrix products: 12.6 us -> none  [the longest x2 5.22 us: decode(): up_part = jnp.dot(scaled, up_weight, preferred_element_type=jnp.float32)]
  transfers between devices with their start and end apart: 1 -> 0, of which waited for: 1 -> 0; matrix products, arithmetic and copies ran while one was open for 0% -> 0% of each run, Pallas kernels for 0% -> 0%
where the time goes in v1:
time: 73.3 us; the launch traced here: 72.7 us
  Pallas kernels  66.6 us (91%)
  local copies, waits for them, and re-layouts  5.23 us (7%)
  between operations  0.8 us (1%)
    pallas_call x1, Pallas kernels, per_device(): pl.pallas_call(kernel, out_shape=[jax.ShapeDtypeStruct((OWN, DL), BF16)]...  66.6 us
    unnamed x23, local copies, waits for them, and re-layouts  5.23 us

profile of v1, /device:TPU:6, one launch (start us, length us, event | category | flops | bytes accessed | tf_op | source)
XLA Modules:
  0.0 72.7 jit_solution(13119155411129146226)
XLA Ops:
  0.6 1.0 %copy.14.dl_ref = bf16[448,64]{1,0:T(8,128)(2,1)S(1)} copy(bf16[448,64]{0,1:T(8,128)(2,1)} %param.22) | data formatting | bytes 114688 | tf_op args[10]
  1.6 1.5 %copy.15.gate_hbm = bf16[1024,448]{1,0:T(8,128)(2,1)S(1)} copy(bf16[1024,448]{0,1:T(8,128)(2,1)} %param.15) | data formatting | bytes 1835008 | tf_op args[3]
  3.1 0.0 copy-start
  3.1 0.0 copy-start.1
  3.1 0.0 copy-start.2
  3.1 0.0 copy-start.3
  3.1 0.0 copy-start.4
  3.1 0.0 copy-start.5
  3.2 0.0 copy-start.6
  3.2 0.0 copy-start.7
  3.2 0.0 copy-start.8
  3.2 1.5 %copy.16.up_hbm = bf16[1024,448]{1,0:T(8,128)(2,1)S(1)} copy(bf16[1024,448]{0,1:T(8,128)(2,1)} %param.16) | data formatting | bytes 1835008 | tf_op args[4]
  4.7 0.0 copy-done
  4.7 0.0 copy-done.1
  4.7 0.0 copy-done.2
  4.8 0.0 copy-done.3
  4.8 0.0 copy-done.4
  4.8 0.0 copy-done.5
  4.8 0.0 copy-done.6
  4.8 0.0 copy-done.7
  4.8 0.0 copy-done.8
  4.8 66.6 %shard_map.131 = (bf16[4,1024]{1,0:T(4,128)(2,1)S(1)}, bf16[4,1024]{1,0:T(4,128)(2,1)S(1)}) custom-call(bf16[4,1024]{1,0:T(4,128)(2,1)S(1)} %copy-done.3, bf16[4,1024]{1,0:T(4,128)(2,1)S(1)} %copy-done.4, f32[1,1024]{1,0:T(1,128)S(1)} %bitcast.1, bf16[16,64]{1,0:T(8,128)(2,1)S(1)} %copy-done.6, bf16[16,64]{1,0:T(8,128)(2,1)S(1)} %copy-done.7, ...), custom_call_target="tpu_custom_call" | custom-call | flops 1585446912 | bytes 2752512 | tf_op jit(solution)/shard_map/pallas_call | solution.py:397
  71.5 0.6 copy.19
  72.1 0.6 copy.20
Async XLA Ops:
  3.1 1.7 %copy-start = (bf16[448,1024]{1,0:T(8,128)(2,1)S(1)}, bf16[448,1024]{1,0:T(8,128)(2,1)}, u32[]{:S(2)}) copy-start(bf16[448,1024]{1,0:T(8,128)(2,1)} %down_hbm.1) | copy-start | bytes 2752516
  3.1 1.6 %copy-start.1 = (bf16[64,448]{1,0:T(8,128)(2,1)S(1)}, bf16[64,448]{1,0:T(8,128)(2,1)}, u32[]{:S(2)}) copy-start(bf16[64,448]{1,0:T(8,128)(2,1)} %gr_ref.1) | copy-start | bytes 172036
  3.1 1.6 %copy-start.2 = (bf16[64,448]{1,0:T(8,128)(2,1)S(1)}, bf16[64,448]{1,0:T(8,128)(2,1)}, u32[]{:S(2)}) copy-start(bf16[64,448]{1,0:T(8,128)(2,1)} %ur_ref.1) | copy-start | bytes 172036
  3.1 1.6 %copy-start.3 = (bf16[4,1024]{1,0:T(4,128)(2,1)S(1)}, bf16[4,1024]{1,0:T(4,128)(2,1)}, u32[]{:S(2)}) copy-start(bf16[4,1024]{1,0:T(4,128)(2,1)} %old_ref.1) | copy-start | bytes 24580
  3.1 1.6 %copy-start.4 = (bf16[4,1024]{1,0:T(4,128)(2,1)S(1)}, bf16[4,1024]{1,0:T(4,128)(2,1)}, u32[]{:S(2)}) copy-start(bf16[4,1024]{1,0:T(4,128)(2,1)} %new_ref.1) | copy-start | bytes 24580
  3.1 1.6 %copy-start.5 = (f32[1024]{0:T(1024)S(1)}, f32[1024]{0:T(1024)}, u32[]{:S(2)}) copy-start(f32[1024]{0:T(1024)} %param.14) | copy-start | bytes 12292
  3.2 1.6 %copy-start.6 = (bf16[16,64]{1,0:T(8,128)(2,1)S(1)}, bf16[16,64]{1,0:T(8,128)(2,1)}, u32[]{:S(2)}) copy-start(bf16[16,64]{1,0:T(8,128)(2,1)} %gl_ref.1) | copy-start | bytes 6148
  3.2 1.6 %copy-start.7 = (bf16[16,64]{1,0:T(8,128)(2,1)S(1)}, bf16[16,64]{1,0:T(8,128)(2,1)}, u32[]{:S(2)}) copy-start(bf16[16,64]{1,0:T(8,128)(2,1)} %ul_ref.1) | copy-start | bytes 6148
  3.2 1.6 %copy-start.8 = (bf16[16,64]{1,0:T(8,128)(2,1)S(1)}, bf16[16,64]{1,0:T(8,128)(2,1)}, u32[]{:S(2)}) copy-start(bf16[16,64]{1,0:T(8,128)(2,1)} %dr_ref.1) | copy-start | bytes 6148

commit v2 on v1

--- a/solution.py
+++ b/solution.py
@@ -33,11 +33,11 @@
 
 
 def kernel(
-    old_ref, new_ref, gain_ref, gl_ref, ul_ref, dr_ref, gr_ref, ur_ref, dl_ref, gate_hbm, up_hbm, down_hbm,
+    old_hbm, new_hbm, gain_hbm, gl_hbm, ul_hbm, dr_hbm, gr_hbm, ur_hbm, dl_hbm, gate_hbm, up_hbm, down_hbm,
     out_old_ref, out_new_ref,
-    gate_v, up_v, down_v, w_old, w_new, down_new, rcomb,
-    s1_old, s1_new, fac, x_old, x_new,
-    p_old, p_new, t_old, t_new, h_old, h_new,
+    old_v, new_v, gain_v, gl_v, ul_v, dr_v, gr_v, ur_v, dl_v, w_in, down_v, down_new,
+    s1_old, s1_new, left, right, x_old, x_new,
+    p_old, p_new, p_low, t_old, t_new, t_low, h_old, h_new,
     d_own, d_sib_old, d_sib_new, e_old, e_new, cs_old, cs_new, r1_old, r1_new, c2_old, c2_new, r2_old, r2_new, inv_new,
     local_sem, ss, rs,
 ):
@@ -53,7 +53,6 @@
         return (zh * 16 + ((y + k) % NY) * 2 + c, t)
 
     counter = [0]
-    pending = {0: [], 1: [], None: []}
 
     def sems(n):
         counter[0] += n
@@ -63,14 +62,6 @@
         return pltpu.make_async_remote_copy(
             src_ref=src, dst_ref=dst, send_sem=ss.at[s], recv_sem=rs.at[r], device_id=dev, device_id_type=MESH
         )
-
-    loads = [
-        pltpu.make_async_copy(gate_hbm, gate_v, local_sem.at[0]),
-        pltpu.make_async_copy(up_hbm, up_v, local_sem.at[1]),
-        pltpu.make_async_copy(down_hbm, down_v, local_sem.at[2]),
-    ]
-    for load in loads:
-        load.start()
 
     barrier = pltpu.get_barrier_semaphore()
     greet = [sibling] + [z_peer(k) for k in Z_ORDER] + [y_peer(k) for k in Y_ORDER]
@@ -78,11 +69,32 @@
     for dev in greet:
         pl.semaphore_signal(barrier, inc=1, device_id=dev, device_id_type=MESH)
 
+    small = [
+        pltpu.make_async_copy(src, dst, local_sem.at[6 + n])
+        for n, (src, dst) in enumerate(
+            ((old_hbm, old_v), (gain_hbm, gain_v), (new_hbm, new_v), (gl_hbm, gl_v), (ul_hbm, ul_v), (dr_hbm, dr_v))
+        )
+    ]
+    for load in small:
+        load.start()
+    loads = [
+        pltpu.make_async_copy(gate_hbm, w_in.at[0:FL], local_sem.at[0]),
+        pltpu.make_async_copy(up_hbm, w_in.at[FL : 2 * FL], local_sem.at[1]),
+        pltpu.make_async_copy(down_hbm, down_v, local_sem.at[2]),
+        pltpu.make_async_copy(gr_hbm, gr_v, local_sem.at[3]),
+        pltpu.make_async_copy(ur_hbm, ur_v, local_sem.at[4]),
+        pltpu.make_async_copy(dl_hbm, dl_v, local_sem.at[5]),
+    ]
+    for load in loads:
+        load.start()
+
     lane = lax.broadcasted_iota(jnp.int32, (OWN, LANES), 1)
     sums = jnp.zeros((OWN, LANES), F32)
-    gain = gain_ref[...]
+    for load in small:
+        load.wait()
+    gain = gain_v[...]
     folded = []
-    for i, ref in enumerate((old_ref, new_ref)):
+    for i, ref in enumerate((old_v, new_v)):
         values = ref[...].astype(F32)
         square = jnp.sum(values * values, axis=1, keepdims=True)
         high = square.astype(BF16).astype(F32)
@@ -92,9 +104,8 @@
     zeros = jnp.zeros((48 - CHUNKS * OWN - OWN, LANES), F32)
     s1_old[0] = jnp.concatenate(folded[0] + [sums, zeros], axis=0).astype(BF16)
     s1_new[0] = jnp.concatenate(folded[1], axis=0).astype(BF16)
-    left = jnp.concatenate([gl_ref[...], ul_ref[...]], axis=1)
-    right = jnp.concatenate([dr_ref[...], jnp.zeros((16, LANES - R), BF16)], axis=1)
-    fac[c, y, zh] = jnp.concatenate([left, right], axis=0)
+    left[c, y, zh] = jnp.concatenate([gl_v[...], ul_v[...]], axis=1)
+    right[c, y, zh] = jnp.concatenate([dr_v[...], jnp.zeros((16, LANES - R), BF16)], axis=1)
 
     pl.semaphore_wait(barrier, len(greet))
 
@@ -112,29 +123,19 @@
         def block(self, k):
             return pl.ds(k * self.rows, self.rows)
 
-        def record(self, copies):
-            pending[self.core] += copies
-            return copies
-
     planes = (Plane(0), Plane(1))
     base = {}
-    for name in ("a1o", "a1n", "a1f", "a2o", "a2n", "a2f", "fo", "fn", "c1o", "c1n", "c2o", "c2n", "to", "tn", "ho", "hn"):
+    for name in ("a1o", "a1n", "a1l", "a1r", "a2o", "a2n", "a2l", "a2r", "fo", "fn", "c1o", "c1n", "c2o", "c2n", "to", "tn", "tl", "ho", "hn"):
         base[name] = sems(8)
-    for name in ("ff", "eo", "en"):
+    for name in ("fl", "fr", "eo", "en"):
         base[name] = sems(1)
 
-    def stage1(pln, name, src, dst_of):
-        return [remote(src, dst_of(k), base[name] + k, base[name] + k, pln.peer1(k)) for k in pln.order1]
-
-    def a1_copies(pln):
-        return (
-            [remote(s1_old.at[0], s1_old.at[k], base["a1o"] + k, base["a1o"] + k, pln.peer1(k)) for k in pln.order1],
-            [remote(s1_new.at[0], s1_new.at[k], base["a1n"] + k, base["a1n"] + k, pln.peer1(k)) for k in pln.order1],
-            [
-                remote(fac.at[c, y, zh], fac.at[c, y, zh], base["a1f"] + k, base["a1f"] + k, pln.peer1(k))
-                for k in pln.order1
-            ],
-        )
+    def a1_copies(pln, name, s1):
+        return [remote(s1.at[0], s1.at[k], base[name] + k, base[name] + k, pln.peer1(k)) for k in pln.order1]
+
+    def a1_factor_copies(pln, name, fac):
+        own = fac.at[c, y, zh]
+        return [remote(own, own, base[name] + k, base[name] + k, z_peer(k)) for k in Z_ORDER]
 
     def a2_copies(pln, name, x_ref):
         return [
@@ -142,9 +143,9 @@
             for k in pln.order2
         ]
 
-    def a2_factor_copies(pln):
-        part = fac.at[c, y] if pln.core == 0 else fac.at[c, :, zh]
-        return [remote(part, part, base["a2f"] + k, base["a2f"] + k, pln.peer2(k)) for k in pln.order2]
+    def a2_factor_copies(pln, name, fac):
+        part = fac.at[c, y]
+        return [remote(part, part, base[name] + k, base[name] + k, y_peer(k)) for k in Y_ORDER]
 
     def forward(pln, name, x_ref, k):
         return remote(x_ref.at[0, pln.block(k)], x_ref.at[1, pln.block(k)], base[name] + k, base[name], sibling)
@@ -160,40 +161,31 @@
             pl.when(c == pln.core)(functools.partial(fn, pln))
 
     def gather_first(pln):
-        olds, news, facs = a1_copies(pln)
-        for copy in olds + news + facs:
+        olds, news = a1_copies(pln, "a1o", s1_old), a1_copies(pln, "a1n", s1_new)
+        lefts, rights = a1_factor_copies(pln, "a1l", left), a1_factor_copies(pln, "a1r", right)
+        seconds = a2_copies(pln, "a2o", x_old)
+        for copy in olds + news:
             copy.start()
         for copy in olds:
             copy.wait_recv()
         assemble(pln, s1_old, x_old, CHUNKS + 1)
-        for copy in a2_copies(pln, "a2o", x_old):
+        for copy in seconds:
             copy.start()
         forward(pln, "fo", x_old, 0).start()
+        for copy in lefts + rights:
+            copy.start()
         for copy in news:
             copy.wait_recv()
         assemble(pln, s1_new, x_new, CHUNKS)
+        for copy in seconds:
+            copy.wait_send()
         for copy in a2_copies(pln, "a2n", x_new):
             copy.start()
         forward(pln, "fn", x_new, 0).start()
-        for copy in facs:
-            copy.wait_recv()
-        for copy in a2_factor_copies(pln):
-            copy.start()
 
     per_core(gather_first)
-
-    loads[0].wait()
-    loads[1].wait()
-
-    def join(i, carry):
-        part = pl.ds(i * 128, 128)
-        w_old[part, :] = jnp.concatenate([gate_v[part, :], up_v[part, :]], axis=1)
-        return carry
-
-    lax.fori_loop(0, DL // 128, join, 0)
-    none = jnp.zeros((R, FL), BF16)
-    rcomb[0:R, :] = jnp.concatenate([gr_ref[...], none], axis=1)
-    rcomb[R : 2 * R, :] = jnp.concatenate([none, ur_ref[...]], axis=1)
+    for load in loads:
+        load.wait()
 
     def gather_second(pln, name, forward_name, x_ref):
         copies = a2_copies(pln, name, x_ref)
@@ -207,8 +199,10 @@
     def reduce_copy(name, p_ref, t_ref, b):
         return remote(p_ref.at[b], t_ref.at[pos], base[name] + b, base[name] + pos, (g, block_target(b)))
 
-    def project(half, x_ref, w_ref, p_ref, t_ref, name, with_sums):
-        product = jnp.dot(x_ref[half, :, 0:DL], w_ref[...], preferred_element_type=F32)
+    def project(half, x_ref, p_ref, t_ref, name, with_sums):
+        product = lax.dot_general(
+            x_ref[half, :, 0:DL], w_in[...], (((1,), (1,)), ((), ())), preferred_element_type=F32
+        )
         p_ref[4 * half : 4 * half + 4, :, 0 : 2 * FL] = product.astype(BF16).reshape(4, BLOCK, 2 * FL)
         if with_sums:
             p_ref[4 * half : 4 * half + 4, :, 2 * FL :] = x_ref[half, :, DL:].reshape(4, BLOCK, LANES)
@@ -233,10 +227,10 @@
             copies.append(remote(h_ref.at[pos], h_ref.at[pos], base[name] + b, base[name] + pos, (g, block_target(b))))
         return copies
 
-    def activate(total, inverse, name, h_ref):
-        gate = total[:, 0:FL] * inverse
-        up = total[:, FL : 2 * FL] * inverse
+    def activate(gate, up, h_ref):
         h_ref[pos] = (gate / (1.0 + jnp.exp(-gate)) * up).astype(BF16)
+
+    def spread(name, h_ref):
         for copy in hidden_copies(name, h_ref):
             copy.start()
 
@@ -297,65 +291,86 @@
         ).astype(BF16)
 
     per_core(lambda pln: gather_second(pln, "a2o", "fo", x_old))
-    project(0, x_old, w_old, p_old, t_old, "to", True)
+    project(0, x_old, p_old, t_old, "to", True)
     wait_sibling_half("fo", x_old)
-    project(1, x_old, w_old, p_old, t_old, "to", True)
-
-    per_core(lambda pln: gather_second(pln, "a2n", "fn", x_new))
-
-    def gather_factors(pln):
-        for copy in a2_factor_copies(pln):
-            copy.wait_recv()
-
-    per_core(gather_factors)
-    plane = fac.at[c]
-    factor_exchange = remote(plane, plane, base["ff"], base["ff"], sibling)
-    factor_exchange.start()
-    factor_exchange.wait_recv()
-    loads[2].wait()
-
-    def merge_in(q):
-        rows = pl.ds(q * 256, 256)
-        left = jnp.concatenate([fac[i % 2, i // 2, q, 0:16, :] for i in range(16)], axis=0)
-        product = jnp.dot(left, rcomb[...], preferred_element_type=F32)
-        w_new[rows, :] = (w_old[rows, :].astype(F32) + ALPHA / R * product).astype(BF16)
-
-    def merge_down(q):
-        columns = pl.ds(q * 256, 256)
-        right = jnp.concatenate([fac[i % 2, i // 2, q, 16:32, 0:R] for i in range(16)], axis=0)
-        product = lax.dot_general(dl_ref[...], right, (((1,), (1,)), ((), ())), preferred_element_type=F32)
-        down_new[:, columns] = (down_v[:, columns].astype(F32) + ALPHA / R * product).astype(BF16)
-
-    for q in range(4):
-        merge_in(q)
-    project(0, x_new, w_new, p_new, t_new, "tn", False)
+    project(1, x_old, p_old, t_old, "to", True)
+
+    def gather_rest(pln):
+        gather_second(pln, "a2n", "fn", x_new)
+        for copy in a2_copies(pln, "a2n", x_new):
+            copy.wait_send()
+        for name1, name2, fac in (("a1l", "a2l", left), ("a1r", "a2r", right)):
+            for copy in a1_factor_copies(pln, name1, fac):
+                copy.wait_recv()
+            for copy in a2_factor_copies(pln, name2, fac):
+                copy.start()
+
+    per_core(gather_rest)
+    for b in range(NT):
+        pl.when(b != pos)(lambda b=b: reduce_copy("to", p_old, t_old, b).wait_send())
+    project(0, x_new, p_new, t_new, "tn", False)
     wait_sibling_half("fn", x_new)
-    project(1, x_new, w_new, p_new, t_new, "tn", False)
+    project(1, x_new, p_new, t_new, "tn", False)
 
     total = reduced(p_old, t_old, "to")
     mean = total[:, 2 * FL :] * (1.0 / D)
     inverse_old = lax.rsqrt(mean[:, 0:1] + mean[:, 1:2] + 1e-05)
     inv_new[...] = jnp.broadcast_to(lax.rsqrt(mean[:, 2:3] + mean[:, 3:4] + 1e-05), (BLOCK, LANES))
-    activate(total, inverse_old, "ho", h_old)
-    for q in range(4):
-        merge_down(q)
+    activate(total[:, 0:FL] * inverse_old, total[:, FL : 2 * FL] * inverse_old, h_old)
+
+    def exchange_factors(name2, name, fac):
+        def wait(pln):
+            for copy in a2_factor_copies(pln, name2, fac):
+                copy.wait_recv()
+
+        per_core(wait)
+        copy = remote(fac.at[c], fac.at[c], base[name], base[name], sibling)
+        copy.start()
+        return copy
+
+    left_exchange = exchange_factors("a2l", "fl", left)
+    left_exchange.wait_recv()
+    low = jnp.zeros((ROWS, 2 * R), F32)
+    for q in range(NZ):
+        part = jnp.concatenate([left[i % 2, i // 2, q] for i in range(2 * NY)], axis=0)
+        columns = x_new[:, :, q * 256 : (q + 1) * 256].reshape(ROWS, 256)
+        low += jnp.dot(columns, part, preferred_element_type=F32)
+    p_low[...] = low.astype(BF16).reshape(NT, BLOCK, 2 * R)
+    for b in range(NT):
+        pl.when(b != pos)(lambda b=b: reduce_copy("tl", p_low, t_low, b).start())
+    right_exchange = exchange_factors("a2r", "fr", right)
+
+    for b in range(NT):
+        pl.when(b != pos)(lambda b=b: reduce_copy("tn", p_new, t_new, b).wait_send())
+    spread("ho", h_old)
+
+    total = reduced(p_new, t_new, "tn")
+    low = reduced(p_low, t_low, "tl").astype(BF16)
+    gate = total[:, 0:FL] + ALPHA / R * jnp.dot(low[:, 0:R], gr_v[...], preferred_element_type=F32)
+    up = total[:, FL : 2 * FL] + ALPHA / R * jnp.dot(low[:, R : 2 * R], ur_v[...], preferred_element_type=F32)
+    activate(gate * inv_new[:, 0:1], up * inv_new[:, 0:1], h_new)
+    spread("hn", h_new)
+    right_exchange.wait_recv()
+    for q in range(NZ):
+        columns = pl.ds(q * 256, 256)
+        part = jnp.concatenate([right[i % 2, i // 2, q, :, 0:R] for i in range(2 * NY)], axis=0)
+        product = lax.dot_general(dl_v[...], part, (((0,), (1,)), ((), ())), preferred_element_type=F32)
+        down_new[:, columns] = (down_v[:, columns].astype(F32) + ALPHA / R * product).astype(BF16)
+
     down_project("ho", h_old, down_v, d_sib_old, e_old, "eo", cs_old)
     per_core(lambda pln: scatter_first(pln, "c1o", cs_old, r1_old))
 
-    total = reduced(p_new, t_new, "tn")
-    activate(total, inv_new[:, 0:1], "hn", h_new)
-    per_core(lambda pln: scatter_second(pln, "c1o", cs_old, r1_old, "c2o", c2_old, r2_old))
     down_project("hn", h_new, down_new, d_sib_new, e_new, "en", cs_new)
     per_core(lambda pln: scatter_first(pln, "c1n", cs_new, r1_new))
+    per_core(lambda pln: scatter_second(pln, "c1o", cs_old, r1_old, "c2o", c2_old, r2_old))
+    per_core(lambda pln: scatter_second(pln, "c1n", cs_new, r1_new, "c2n", c2_new, r2_new))
     per_core(lambda pln: scatter_last(pln, "c2o", c2_old, r2_old, out_old_ref))
-    per_core(lambda pln: scatter_second(pln, "c1n", cs_new, r1_new, "c2n", c2_new, r2_new))
     per_core(lambda pln: scatter_last(pln, "c2n", c2_new, r2_new, out_new_ref))
 
     def drain(pln):
-        for group in a1_copies(pln):
-            for copy in group:
-                copy.wait_send()
-        copies = a2_copies(pln, "a2o", x_old) + a2_copies(pln, "a2n", x_new) + a2_factor_copies(pln)
+        copies = a1_copies(pln, "a1o", s1_old) + a1_copies(pln, "a1n", s1_new)
+        copies += a1_factor_copies(pln, "a1l", left) + a1_factor_copies(pln, "a1r", right)
+        copies += a2_factor_copies(pln, "a2l", left) + a2_factor_copies(pln, "a2r", right)
         copies += [forward(pln, "fo", x_old, k) for k in range(pln.n2)]
         copies += [forward(pln, "fn", x_new, k) for k in range(pln.n2)]
         copies += c1_copies(pln, "c1o", cs_old, r1_old) + c1_copies(pln, "c1n", cs_new, r1_new)
@@ -364,13 +379,13 @@
             copy.wait_send()
 
     per_core(drain)
-    factor_exchange.wait_send()
+    left_exchange.wait_send()
+    right_exchange.wait_send()
     remote(d_sib_old, e_old, base["eo"], base["eo"], sibling).wait_send()
     remote(d_sib_new, e_new, base["en"], base["en"], sibling).wait_send()
     for b in range(NT):
         def wait(b=b):
-            reduce_copy("to", p_old, t_old, b).wait_send()
-            reduce_copy("tn", p_new, t_new, b).wait_send()
+            reduce_copy("tl", p_low, t_low, b).wait_send()
         pl.when(b != pos)(wait)
     for copy in hidden_copies("ho", h_old) + hidden_copies("hn", h_new):
         copy.wait_send()
@@ -380,12 +395,15 @@
     vmem = pl.BlockSpec(memory_space=pltpu.VMEM)
     hbm = pl.BlockSpec(memory_space=pl.ANY)
     scratch = [
-        ((DL, FL), BF16), ((DL, FL), BF16), ((FL, DL), BF16),
-        ((DL, 2 * FL), BF16), ((DL, 2 * FL), BF16), ((FL, DL), BF16), ((2 * R, 2 * FL), BF16),
-        ((8, 48, LANES), BF16), ((8, 32, LANES), BF16), ((2, NY, NZ, 32, LANES), BF16),
+        ((OWN, DL), BF16), ((OWN, DL), BF16), ((1, DL), F32),
+        ((16, R), BF16), ((16, R), BF16), ((16, R), BF16),
+        ((R, FL), BF16), ((R, FL), BF16), ((R, FL), BF16),
+        ((2 * FL, DL), BF16), ((FL, DL), BF16), ((FL, DL), BF16),
+        ((8, 48, LANES), BF16), ((8, 32, LANES), BF16),
+        ((2, NY, NZ, 16, LANES), BF16), ((2, NY, NZ, 16, LANES), BF16),
         ((2, HALF, DL + LANES), BF16), ((2, HALF, DL), BF16),
-        ((NT, BLOCK, 2 * FL + LANES), BF16), ((NT, BLOCK, 2 * FL), BF16),
-        ((NT, BLOCK, 2 * FL + LANES), BF16), ((NT, BLOCK, 2 * FL), BF16),
+        ((NT, BLOCK, 2 * FL + LANES), BF16), ((NT, BLOCK, 2 * FL), BF16), ((NT, BLOCK, 2 * R), BF16),
+        ((NT, BLOCK, 2 * FL + LANES), BF16), ((NT, BLOCK, 2 * FL), BF16), ((NT, BLOCK, 2 * R), BF16),
         ((NT, BLOCK, FL), BF16), ((NT, BLOCK, FL), BF16),
         ((HALF, DL), F32), ((HALF, DL), BF16), ((HALF, DL), BF16),
         ((HALF, DL), BF16), ((HALF, DL), BF16), ((HALF, DL), BF16), ((HALF, DL), BF16),
@@ -397,15 +415,15 @@
     return pl.pallas_call(
         kernel,
         out_shape=[jax.ShapeDtypeStruct((OWN, DL), BF16)] * 2,
-        in_specs=[vmem] * 9 + [hbm] * 3,
+        in_specs=[hbm] * 12,
         out_specs=[vmem, vmem],
         scratch_shapes=[pltpu.VMEM(shape, dtype) for shape, dtype in scratch]
-        + [pltpu.SemaphoreType.DMA((3,)), pltpu.SemaphoreType.DMA((132,)), pltpu.SemaphoreType.DMA((132,))],
+        + [pltpu.SemaphoreType.DMA((12,)), pltpu.SemaphoreType.DMA((156,)), pltpu.SemaphoreType.DMA((156,))],
         compiler_params=pltpu.CompilerParams(
-            collective_id=0, has_side_effects=True, vmem_limit_bytes=48 * 1024 * 1024
+            collective_id=0, has_side_effects=True, vmem_limit_bytes=60 * 1024 * 1024
         ),
         cost_estimate=pl.CostEstimate(flops=flops, bytes_accessed=6 * DL * FL, transcendentals=2 * BLOCK * FL),
-    )(old, new, gain.reshape(1, DL), gl, ul, dr, gr, ur, dl, gate, up, down)
+    )(old, new, gain.reshape(1, DL), gl, ul, dr, gr, ur, dl.T, gate.T, up.T, down)
 
 
 def solution(mesh):

time: 73.3 us -> 68.4 us (0.933)
  local copies, waits for them, and re-layouts: 5.23 us -> 1.91 us
  Pallas kernels: 66.6 us -> 65.7 us
    unnamed x23 -> x4, local copies, waits for them, and re-layouts: 5.23 us -> 1.91 us
    pallas_call x1, Pallas kernels: 66.6 us -> 65.7 us  [per_device(): pl.pallas_call(kernel, out_shape=[jax.ShapeDtypeStruct((OWN, DL), BF16)]...]
where the time goes in v2:
time: 68.4 us; the launch traced here: 68.3 us
  Pallas kernels  65.7 us (96%)
  local copies, waits for them, and re-layouts  1.91 us (3%)
    pallas_call x1, Pallas kernels, per_device(): pl.pallas_call(kernel, out_shape=[jax.ShapeDtypeStruct((OWN, DL), BF16)]...  65.7 us
    unnamed x4, local copies, waits for them, and re-layouts  1.91 us

profile of v2, /device:TPU:6, one launch (start us, length us, event | category | flops | bytes accessed | tf_op | source)
XLA Modules:
  0.0 68.3 jit_solution(5765398548272098540)
XLA Ops:
  0.6 65.7 %shard_map.131 = (bf16[4,1024]{1,0:T(4,128)(2,1)}, bf16[4,1024]{1,0:T(4,128)(2,1)}) custom-call(bf16[4,1024]{1,0:T(4,128)(2,1)} %old_hbm.1, bf16[4,1024]{1,0:T(4,128)(2,1)} %new_hbm.1, f32[1,1024]{1,0:T(1,128)} %bitcast.7, bf16[16,64]{1,0:T(8,128)(2,1)} %gl_hbm.1, bf16[16,64]{1,0:T(8,128)(2,1)} %ul_hbm.1, bf16[16,64]{1,0:T(8,128)(2,1)} %dr_hbm.1, ...), custom_call_target="tpu_custom_call" | custom-call | flops 1585446912 | bytes 2752512 | tf_op jit(solution)/shard_map/pallas_call | solution.py:415
  66.4 0.0 copy-start
  66.4 1.3 %copy.16 = bf16[4,1024]{1,0:T(4,128)(2,1)} copy(bf16[4,1024]{1,0:T(4,128)(2,1)} %get-tuple-element.4) | data formatting | bytes 16384
  67.7 0.0 copy-done
  67.7 0.6 copy.17
Async XLA Ops:
  66.4 1.3 %copy-start = (bf16[4,1024]{1,0:T(4,128)(2,1)S(1)}, bf16[4,1024]{1,0:T(4,128)(2,1)}, u32[]{:S(2)}) copy-start(bf16[4,1024]{1,0:T(4,128)(2,1)} %get-tuple-element.5) | copy-start | bytes 24580

commit v3 on v2

--- a/solution.py
+++ b/solution.py
@@ -17,6 +17,7 @@
 ROWS, OWN = 256, 4
 HALF = ROWS // 2
 BLOCK = ROWS // NT
+PIECE = HALF // 2
 LANES = 128
 CHUNKS = DL // LANES
 Z_ORDER = (2, 1, 3)
@@ -38,7 +39,7 @@
     old_v, new_v, gain_v, gl_v, ul_v, dr_v, gr_v, ur_v, dl_v, w_in, down_v, down_new,
     s1_old, s1_new, left, right, x_old, x_new,
     p_old, p_new, p_low, t_old, t_new, t_low, h_old, h_new,
-    d_own, d_sib_old, d_sib_new, e_old, e_new, cs_old, cs_new, r1_old, r1_new, c2_old, c2_new, r2_old, r2_new, inv_new,
+    d_sib_old, d_sib_new, e_old, e_new, cs_old, cs_new, r1_old, r1_new, c2_old, c2_new, r2_old, r2_new, square,
     local_sem, ss, rs,
 ):
     g, t = lax.axis_index("groups"), lax.axis_index("tensor")
@@ -88,24 +89,16 @@
     for load in loads:
         load.start()
 
+    def scaled(ref):
+        return fold(ref[...].astype(F32) * gain_v[...])
+
+    for load in small[:3]:
+        load.wait()
+    s1_old[0] = jnp.concatenate(scaled(old_v), axis=0).astype(BF16)
     lane = lax.broadcasted_iota(jnp.int32, (OWN, LANES), 1)
-    sums = jnp.zeros((OWN, LANES), F32)
-    for load in small:
-        load.wait()
-    gain = gain_v[...]
-    folded = []
-    for i, ref in enumerate((old_v, new_v)):
-        values = ref[...].astype(F32)
-        square = jnp.sum(values * values, axis=1, keepdims=True)
-        high = square.astype(BF16).astype(F32)
-        sums = jnp.where(lane == 2 * i, high, sums)
-        sums = jnp.where(lane == 2 * i + 1, square - high, sums)
-        folded.append(fold(values * gain))
-    zeros = jnp.zeros((48 - CHUNKS * OWN - OWN, LANES), F32)
-    s1_old[0] = jnp.concatenate(folded[0] + [sums, zeros], axis=0).astype(BF16)
-    s1_new[0] = jnp.concatenate(folded[1], axis=0).astype(BF16)
-    left[c, y, zh] = jnp.concatenate([gl_v[...], ul_v[...]], axis=1)
-    right[c, y, zh] = jnp.concatenate([dr_v[...], jnp.zeros((16, LANES - R), BF16)], axis=1)
+    squares = [jnp.sum(ref[...].astype(F32) ** 2, axis=1, keepdims=True) for ref in (old_v, new_v)]
+    squares = jnp.where(lane == 0, squares[0], jnp.where(lane == 1, squares[1], 0.0))
+    square[pos] = jnp.concatenate([squares, jnp.zeros((8 - OWN, LANES), F32)], axis=0)
 
     pl.semaphore_wait(barrier, len(greet))
 
@@ -125,10 +118,10 @@
 
     planes = (Plane(0), Plane(1))
     base = {}
-    for name in ("a1o", "a1n", "a1l", "a1r", "a2o", "a2n", "a2l", "a2r", "fo", "fn", "c1o", "c1n", "c2o", "c2n", "to", "tn", "tl", "ho", "hn"):
+    for name in ("a1o", "a1n", "a1l", "a1r", "a2o", "a2n", "a2l", "a2r", "fo", "fn", "c1o", "c1n", "c2o", "c2n", "to", "tn", "tl", "ho", "hn", "sq"):
         base[name] = sems(8)
     for name in ("fl", "fr", "eo", "en"):
-        base[name] = sems(1)
+        base[name] = sems(2)
 
     def a1_copies(pln, name, s1):
         return [remote(s1.at[0], s1.at[k], base[name] + k, base[name] + k, pln.peer1(k)) for k in pln.order1]
@@ -160,19 +153,53 @@
         for pln in planes:
             pl.when(c == pln.core)(functools.partial(fn, pln))
 
+    def hidden_copies(name, h_ref):
+        copies = []
+        for k in (6, 2, 5, 3, 7, 1, 4):
+            b = (pos + k) % NT
+            copies.append(remote(h_ref.at[pos], h_ref.at[pos], base[name] + b, base[name] + pos, (g, block_target(b))))
+        return copies
+
+    def wait_hidden(name, h_ref, blocks):
+        for b in blocks:
+            def wait(b=b):
+                remote(h_ref.at[b], h_ref.at[b], base[name] + b, base[name] + b, (g, block_target(b))).wait_recv()
+            pl.when(b != pos)(wait)
+
     def gather_first(pln):
         olds, news = a1_copies(pln, "a1o", s1_old), a1_copies(pln, "a1n", s1_new)
         lefts, rights = a1_factor_copies(pln, "a1l", left), a1_factor_copies(pln, "a1r", right)
         seconds = a2_copies(pln, "a2o", x_old)
-        for copy in olds + news:
-            copy.start()
+        for copy in olds + hidden_copies("sq", square):
+            copy.start()
+        s1_new[0] = jnp.concatenate(scaled(new_v), axis=0).astype(BF16)
+        for copy in news:
+            copy.start()
+        for load in small[3:]:
+            load.wait()
+        left[c, y, zh] = jnp.concatenate([gl_v[...], ul_v[...]], axis=1)
         for copy in olds:
             copy.wait_recv()
-        assemble(pln, s1_old, x_old, CHUNKS + 1)
+        assemble(pln, s1_old, x_old, CHUNKS)
         for copy in seconds:
             copy.start()
         forward(pln, "fo", x_old, 0).start()
-        for copy in lefts + rights:
+        for copy in lefts:
+            copy.start()
+        wait_hidden("sq", square, range(NT))
+        total = square[0]
+        for b in range(1, NT):
+            total += square[b]
+        inverse = lax.rsqrt(total * (1.0 / D) + 1e-05)
+        high = inverse.astype(BF16).astype(F32)
+        low = inverse - high
+        lane = lax.broadcasted_iota(jnp.int32, (8, LANES - R), 1)
+        beside = jnp.zeros((8, LANES - R), F32)
+        for n, column in enumerate((high[:, 0:1], low[:, 0:1], high[:, 1:2], low[:, 1:2])):
+            beside = jnp.where(lane == n, column, beside)
+        beside = jnp.concatenate([beside, jnp.zeros((8, LANES - R), F32)], axis=0)
+        right[c, y, zh] = jnp.concatenate([dr_v[...].astype(F32), beside], axis=1).astype(BF16)
+        for copy in rights:
             copy.start()
         for copy in news:
             copy.wait_recv()
@@ -199,13 +226,11 @@
     def reduce_copy(name, p_ref, t_ref, b):
         return remote(p_ref.at[b], t_ref.at[pos], base[name] + b, base[name] + pos, (g, block_target(b)))
 
-    def project(half, x_ref, p_ref, t_ref, name, with_sums):
+    def project(half, x_ref, p_ref, t_ref, name):
         product = lax.dot_general(
             x_ref[half, :, 0:DL], w_in[...], (((1,), (1,)), ((), ())), preferred_element_type=F32
         )
         p_ref[4 * half : 4 * half + 4, :, 0 : 2 * FL] = product.astype(BF16).reshape(4, BLOCK, 2 * FL)
-        if with_sums:
-            p_ref[4 * half : 4 * half + 4, :, 2 * FL :] = x_ref[half, :, DL:].reshape(4, BLOCK, LANES)
         for b in range(4 * half, 4 * half + 4):
             pl.when(b != pos)(lambda b=b: reduce_copy(name, p_ref, t_ref, b).start())
 
@@ -220,38 +245,12 @@
             total += t_ref[b].astype(F32)
         return total
 
-    def hidden_copies(name, h_ref):
-        copies = []
-        for k in (6, 2, 5, 3, 7, 1, 4):
-            b = (pos + k) % NT
-            copies.append(remote(h_ref.at[pos], h_ref.at[pos], base[name] + b, base[name] + pos, (g, block_target(b))))
-        return copies
-
     def activate(gate, up, h_ref):
         h_ref[pos] = (gate / (1.0 + jnp.exp(-gate)) * up).astype(BF16)
 
     def spread(name, h_ref):
         for copy in hidden_copies(name, h_ref):
             copy.start()
-
-    def wait_hidden(name, h_ref, half):
-        for b in range(4 * half, 4 * half + 4):
-            def wait(b=b):
-                remote(h_ref.at[b], h_ref.at[b], base[name] + b, base[name] + b, (g, block_target(b))).wait_recv()
-            pl.when(b != pos)(wait)
-
-    def down_project(h_name, h_ref, down_ref, d_sib, e_ref, e_name, cs_ref):
-        wait_hidden(h_name, h_ref, 1)
-        d_sib[...] = jnp.dot(
-            h_ref[4:8].reshape(HALF, FL), down_ref[...], preferred_element_type=F32
-        ).astype(BF16)
-        exchange = remote(d_sib, e_ref, base[e_name], base[e_name], sibling)
-        exchange.start()
-        wait_hidden(h_name, h_ref, 0)
-        d_own[...] = jnp.dot(h_ref[0:4].reshape(HALF, FL), down_ref[...], preferred_element_type=F32)
-        exchange.wait_recv()
-        d_own[...] += e_ref[...].astype(F32)
-        cs_ref[...] = d_own[...].astype(BF16)
 
     def c1_copies(pln, name, cs_ref, r1_ref):
         return [
@@ -264,9 +263,34 @@
             remote(c2_ref.at[k], r2_ref.at[k], base[name] + k, base[name] + k, pln.peer1(-k)) for k in pln.order1
         ]
 
-    def scatter_first(pln, name, cs_ref, r1_ref):
-        for copy in c1_copies(pln, name, cs_ref, r1_ref):
-            copy.start()
+    def exchange_piece(name, d_sib, e_ref, piece):
+        rows = pl.ds(piece * PIECE, PIECE)
+        return remote(d_sib.at[rows], e_ref.at[rows], base[name] + piece, base[name] + piece, sibling)
+
+    def down_project(h_name, h_ref, down_ref, d_sib, e_ref, e_name, cs_ref, c1_name, r1_ref):
+        def product(half, piece):
+            first = 4 * half + 2 * piece
+            wait_hidden(h_name, h_ref, (first, first + 1))
+            return jnp.dot(
+                h_ref[first : first + 2].reshape(PIECE, FL), down_ref[...], preferred_element_type=F32
+            )
+
+        for piece in (1, 0):
+            d_sib[piece * PIECE : (piece + 1) * PIECE] = product(1, piece).astype(BF16)
+            exchange_piece(e_name, d_sib, e_ref, piece).start()
+        for piece in (1, 0):
+            rows = pl.ds(piece * PIECE, PIECE)
+            own = product(0, piece)
+            exchange_piece(e_name, d_sib, e_ref, piece).wait_recv()
+            cs_ref[rows] = (own + e_ref[rows].astype(F32)).astype(BF16)
+
+            def start(pln, piece=piece):
+                n = PIECE // pln.rows
+                for k, copy in zip(pln.order2, c1_copies(pln, c1_name, cs_ref, r1_ref)):
+                    if k // n == piece:
+                        copy.start()
+
+            per_core(start)
 
     def scatter_second(pln, name1, cs_ref, r1_ref, name2, c2_ref, r2_ref):
         for copy in c1_copies(pln, name1, cs_ref, r1_ref):
@@ -291,9 +315,9 @@
         ).astype(BF16)
 
     per_core(lambda pln: gather_second(pln, "a2o", "fo", x_old))
-    project(0, x_old, p_old, t_old, "to", True)
+    project(0, x_old, p_old, t_old, "to")
     wait_sibling_half("fo", x_old)
-    project(1, x_old, p_old, t_old, "to", True)
+    project(1, x_old, p_old, t_old, "to")
 
     def gather_rest(pln):
         gather_second(pln, "a2n", "fn", x_new)
@@ -308,15 +332,9 @@
     per_core(gather_rest)
     for b in range(NT):
         pl.when(b != pos)(lambda b=b: reduce_copy("to", p_old, t_old, b).wait_send())
-    project(0, x_new, p_new, t_new, "tn", False)
+    project(0, x_new, p_new, t_new, "tn")
     wait_sibling_half("fn", x_new)
-    project(1, x_new, p_new, t_new, "tn", False)
-
-    total = reduced(p_old, t_old, "to")
-    mean = total[:, 2 * FL :] * (1.0 / D)
-    inverse_old = lax.rsqrt(mean[:, 0:1] + mean[:, 1:2] + 1e-05)
-    inv_new[...] = jnp.broadcast_to(lax.rsqrt(mean[:, 2:3] + mean[:, 3:4] + 1e-05), (BLOCK, LANES))
-    activate(total[:, 0:FL] * inverse_old, total[:, FL : 2 * FL] * inverse_old, h_old)
+    project(1, x_new, p_new, t_new, "tn")
 
     def exchange_factors(name2, name, fac):
         def wait(pln):
@@ -340,6 +358,19 @@
         pl.when(b != pos)(lambda b=b: reduce_copy("tl", p_low, t_low, b).start())
     right_exchange = exchange_factors("a2r", "fr", right)
 
+    total = reduced(p_old, t_old, "to")
+    right_exchange.wait_recv()
+    core, i = c + (1 - 2 * c) * (pos // 4), pos % 4
+    rows = []
+    for n in range(8):
+        ky = (1 - core) * (2 * i + n // 4) + core * n
+        kz = (1 - core) * (n % 4) + core * i
+        rows.append(right[core, (y - ky + NY) % NY, (zh - kz + NZ) % NZ].astype(F32)[0:OWN])
+    inverse = jnp.concatenate(rows, axis=0)
+    inverse_old = inverse[:, R : R + 1] + inverse[:, R + 1 : R + 2]
+    inverse_new = inverse[:, R + 2 : R + 3] + inverse[:, R + 3 : R + 4]
+    activate(total[:, 0:FL] * inverse_old, total[:, FL : 2 * FL] * inverse_old, h_old)
+
     for b in range(NT):
         pl.when(b != pos)(lambda b=b: reduce_copy("tn", p_new, t_new, b).wait_send())
     spread("ho", h_old)
@@ -348,24 +379,20 @@
     low = reduced(p_low, t_low, "tl").astype(BF16)
     gate = total[:, 0:FL] + ALPHA / R * jnp.dot(low[:, 0:R], gr_v[...], preferred_element_type=F32)
     up = total[:, FL : 2 * FL] + ALPHA / R * jnp.dot(low[:, R : 2 * R], ur_v[...], preferred_element_type=F32)
-    activate(gate * inv_new[:, 0:1], up * inv_new[:, 0:1], h_new)
+    activate(gate * inverse_new, up * inverse_new, h_new)
     spread("hn", h_new)
-    right_exchange.wait_recv()
     for q in range(NZ):
         columns = pl.ds(q * 256, 256)
         part = jnp.concatenate([right[i % 2, i // 2, q, :, 0:R] for i in range(2 * NY)], axis=0)
         product = lax.dot_general(dl_v[...], part, (((0,), (1,)), ((), ())), preferred_element_type=F32)
         down_new[:, columns] = (down_v[:, columns].astype(F32) + ALPHA / R * product).astype(BF16)
 
-    down_project("ho", h_old, down_v, d_sib_old, e_old, "eo", cs_old)
-    per_core(lambda pln: scatter_first(pln, "c1o", cs_old, r1_old))
-
-    down_project("hn", h_new, down_new, d_sib_new, e_new, "en", cs_new)
-    per_core(lambda pln: scatter_first(pln, "c1n", cs_new, r1_new))
+    down_project("ho", h_old, down_v, d_sib_old, e_old, "eo", cs_old, "c1o", r1_old)
+
+    down_project("hn", h_new, down_new, d_sib_new, e_new, "en", cs_new, "c1n", r1_new)
     per_core(lambda pln: scatter_second(pln, "c1o", cs_old, r1_old, "c2o", c2_old, r2_old))
     per_core(lambda pln: scatter_second(pln, "c1n", cs_new, r1_new, "c2n", c2_new, r2_new))
     per_core(lambda pln: scatter_last(pln, "c2o", c2_old, r2_old, out_old_ref))
-    per_core(lambda pln: scatter_last(pln, "c2n", c2_new, r2_new, out_new_ref))
 
     def drain(pln):
         copies = a1_copies(pln, "a1o", s1_old) + a1_copies(pln, "a1n", s1_new)
@@ -381,14 +408,28 @@
     per_core(drain)
     left_exchange.wait_send()
     right_exchange.wait_send()
-    remote(d_sib_old, e_old, base["eo"], base["eo"], sibling).wait_send()
-    remote(d_sib_new, e_new, base["en"], base["en"], sibling).wait_send()
+    for piece in (1, 0):
+        exchange_piece("eo", d_sib_old, e_old, piece).wait_send()
+        exchange_piece("en", d_sib_new, e_new, piece).wait_send()
     for b in range(NT):
         def wait(b=b):
             reduce_copy("tl", p_low, t_low, b).wait_send()
         pl.when(b != pos)(wait)
-    for copy in hidden_copies("ho", h_old) + hidden_copies("hn", h_new):
+    for copy in hidden_copies("sq", square) + hidden_copies("ho", h_old) + hidden_copies("hn", h_new):
         copy.wait_send()
+
+    per_core(lambda pln: scatter_last(pln, "c2n", c2_new, r2_new, out_new_ref))
+
+
+def hand_over(old_ref, new_ref, out_old_ref, out_new_ref, sem):
+    copies = [
+        pltpu.make_async_copy(old_ref, out_old_ref, sem.at[0]),
+        pltpu.make_async_copy(new_ref, out_new_ref, sem.at[1]),
+    ]
+    for copy in copies:
+        copy.start()
+    for copy in copies:
+        copy.wait()
 
 
 def per_device(old, new, gain, gate, up, down, gl, gr, ul, ur, dl, dr):
@@ -399,31 +440,39 @@
         ((16, R), BF16), ((16, R), BF16), ((16, R), BF16),
         ((R, FL), BF16), ((R, FL), BF16), ((R, FL), BF16),
         ((2 * FL, DL), BF16), ((FL, DL), BF16), ((FL, DL), BF16),
-        ((8, 48, LANES), BF16), ((8, 32, LANES), BF16),
+        ((8, 32, LANES), BF16), ((8, 32, LANES), BF16),
         ((2, NY, NZ, 16, LANES), BF16), ((2, NY, NZ, 16, LANES), BF16),
-        ((2, HALF, DL + LANES), BF16), ((2, HALF, DL), BF16),
-        ((NT, BLOCK, 2 * FL + LANES), BF16), ((NT, BLOCK, 2 * FL), BF16), ((NT, BLOCK, 2 * R), BF16),
-        ((NT, BLOCK, 2 * FL + LANES), BF16), ((NT, BLOCK, 2 * FL), BF16), ((NT, BLOCK, 2 * R), BF16),
+        ((2, HALF, DL), BF16), ((2, HALF, DL), BF16),
+        ((NT, BLOCK, 2 * FL), BF16), ((NT, BLOCK, 2 * FL), BF16), ((NT, BLOCK, 2 * R), BF16),
+        ((NT, BLOCK, 2 * FL), BF16), ((NT, BLOCK, 2 * FL), BF16), ((NT, BLOCK, 2 * R), BF16),
         ((NT, BLOCK, FL), BF16), ((NT, BLOCK, FL), BF16),
-        ((HALF, DL), F32), ((HALF, DL), BF16), ((HALF, DL), BF16),
+        ((HALF, DL), BF16), ((HALF, DL), BF16),
         ((HALF, DL), BF16), ((HALF, DL), BF16), ((HALF, DL), BF16), ((HALF, DL), BF16),
         ((HALF, DL), BF16), ((HALF, DL), BF16),
         ((8, 32, LANES), BF16), ((8, 32, LANES), BF16), ((8, 32, LANES), BF16), ((8, 32, LANES), BF16),
-        ((BLOCK, LANES), F32),
+        ((NT, 8, LANES), F32),
     ]
     flops = 2 * (2 * ROWS * DL * FL * 3 + 3 * DL * FL * R)
-    return pl.pallas_call(
+    out_shape = [jax.ShapeDtypeStruct((OWN, DL), BF16)] * 2
+    outs = pl.pallas_call(
         kernel,
-        out_shape=[jax.ShapeDtypeStruct((OWN, DL), BF16)] * 2,
+        out_shape=out_shape,
         in_specs=[hbm] * 12,
         out_specs=[vmem, vmem],
         scratch_shapes=[pltpu.VMEM(shape, dtype) for shape, dtype in scratch]
-        + [pltpu.SemaphoreType.DMA((12,)), pltpu.SemaphoreType.DMA((156,)), pltpu.SemaphoreType.DMA((156,))],
+        + [pltpu.SemaphoreType.DMA((12,)), pltpu.SemaphoreType.DMA((168,)), pltpu.SemaphoreType.DMA((168,))],
         compiler_params=pltpu.CompilerParams(
             collective_id=0, has_side_effects=True, vmem_limit_bytes=60 * 1024 * 1024
         ),
         cost_estimate=pl.CostEstimate(flops=flops, bytes_accessed=6 * DL * FL, transcendentals=2 * BLOCK * FL),
     )(old, new, gain.reshape(1, DL), gl, ul, dr, gr, ur, dl.T, gate.T, up.T, down)
+    return pl.pallas_call(
+        hand_over,
+        out_shape=out_shape,
+        in_specs=[hbm, hbm],
+        out_specs=[hbm, hbm],
+        scratch_shapes=[pltpu.SemaphoreType.DMA((2,))],
+    )(*outs)
 
 
 def solution(mesh):

time: 68.4 us -> 66.6 us (0.974)
  local copies, waits for them, and re-layouts: 1.91 us -> 0 us
    unnamed x4 -> x0, local copies, waits for them, and re-layouts: 1.91 us -> none
    pallas_call x1 -> x2, Pallas kernels: 65.7 us -> 65.8 us  [the longest x1 64.2 us: per_device(): pl.pallas_call(kernel, out_shape=out_shape, in_specs=[hbm] * 12, out_spec...]
where the time goes in v3:
time: 66.6 us; the launch traced here: 66.5 us
  Pallas kernels  65.8 us (99%)
    pallas_call x1, Pallas kernels, per_device(): pl.pallas_call(kernel, out_shape=out_shape, in_specs=[hbm] * 12, out_spec...  64.2 us
    pallas_call x1, Pallas kernels, per_device(): pl.pallas_call(hand_over, out_shape=out_shape, in_specs=[hbm, hbm], out_s...  1.62 us

profile of v3, /device:TPU:6, one launch (start us, length us, event | category | flops | bytes accessed | tf_op | source)
XLA Modules:
  0.0 66.5 jit_solution(2280975256514294664)
XLA Ops:
  0.6 64.2 %shard_map.131 = (bf16[4,1024]{1,0:T(4,128)(2,1)}, bf16[4,1024]{1,0:T(4,128)(2,1)}) custom-call(bf16[4,1024]{1,0:T(4,128)(2,1)} %old_hbm.1, bf16[4,1024]{1,0:T(4,128)(2,1)} %new_hbm.1, f32[1,1024]{1,0:T(1,128)} %bitcast.7, bf16[16,64]{1,0:T(8,128)(2,1)} %gl_hbm.1, bf16[16,64]{1,0:T(8,128)(2,1)} %ul_hbm.1, bf16[16,64]{1,0:T(8,128)(2,1)} %dr_hbm.1, ...), custom_call_target="tpu_custom_call" | custom-call | flops 1585446912 | bytes 2752512 | tf_op jit(solution)/shard_map/pallas_call | solution.py:457
  64.9 1.6 %shard_map.132 = (bf16[4,1024]{1,0:T(4,128)(2,1)}, bf16[4,1024]{1,0:T(4,128)(2,1)}) custom-call(bf16[4,1024]{1,0:T(4,128)(2,1)} %get-tuple-element.4.old_ref, bf16[4,1024]{1,0:T(4,128)(2,1)} %get-tuple-element.5.new_ref), custom_call_target="tpu_custom_call" | custom-call | tf_op jit(solution)/shard_map/pallas_call | solution.py:469

commit v4 on v3

--- a/solution.py
+++ b/solution.py
@@ -155,8 +155,9 @@
 
     def hidden_copies(name, h_ref):
         copies = []
-        for k in (6, 2, 5, 3, 7, 1, 4):
-            b = (pos + k) % NT
+        for dx, dz in ((2, 1), (2, 0), (1, 0), (3, 1), (3, 0), (1, 1), (0, 1)):
+            x = (t // 2 + dx) % 4
+            b = x + 4 * ((t + dz + x) % 2)
             copies.append(remote(h_ref.at[pos], h_ref.at[pos], base[name] + b, base[name] + pos, (g, block_target(b))))
         return copies
 
@@ -298,11 +299,14 @@
         total = cs_ref[pln.block(0)].astype(F32)
         for k in range(1, pln.n2):
             total += r1_ref[pln.block(k)].astype(F32)
-        for k in range(pln.n1):
+        def put(k):
             piece = jnp.concatenate(fold(total[OWN * k : OWN * (k + 1)]), axis=0)
             c2_ref[k] = piece.astype(BF16)
-        for copy in c2_copies(pln, name2, c2_ref, r2_ref):
-            copy.start()
+
+        for k, copy in zip(pln.order1, c2_copies(pln, name2, c2_ref, r2_ref)):
+            put(k)
+            copy.start()
+        put(0)
 
     def scatter_last(pln, name2, c2_ref, r2_ref, out_ref):
         for copy in c2_copies(pln, name2, c2_ref, r2_ref):
@@ -469,7 +473,7 @@
     return pl.pallas_call(
         hand_over,
         out_shape=out_shape,
-        in_specs=[hbm, hbm],
+        in_specs=[vmem, vmem],
         out_specs=[hbm, hbm],
         scratch_shapes=[pltpu.SemaphoreType.DMA((2,))],
     )(*outs)

time: 66.6 us -> 66.3 us (level)
  no operation moved by 1% of the time
where the time goes in v4:
time: 66.3 us; the launch traced here: 66 us
  Pallas kernels  65.4 us (99%)
    pallas_call x1, Pallas kernels, per_device(): pl.pallas_call(kernel, out_shape=out_shape, in_specs=[hbm] * 12, out_spec...  64.1 us
    pallas_call x1, Pallas kernels, per_device(): pl.pallas_call(hand_over, out_shape=out_shape, in_specs=[vmem, vmem], out...  1.33 us

profile of v4, /device:TPU:6, one launch (start us, length us, event | category | flops | bytes accessed | tf_op | source)
XLA Modules:
  0.0 66.0 jit_solution(11175500757351505521)
XLA Ops:
  0.6 64.1 %shard_map.131 = (bf16[4,1024]{1,0:T(4,128)(2,1)}, bf16[4,1024]{1,0:T(4,128)(2,1)}) custom-call(bf16[4,1024]{1,0:T(4,128)(2,1)} %old_hbm.1, bf16[4,1024]{1,0:T(4,128)(2,1)} %new_hbm.1, f32[1,1024]{1,0:T(1,128)} %bitcast.7, bf16[16,64]{1,0:T(8,128)(2,1)} %gl_hbm.1, bf16[16,64]{1,0:T(8,128)(2,1)} %ul_hbm.1, bf16[16,64]{1,0:T(8,128)(2,1)} %dr_hbm.1, ...), custom_call_target="tpu_custom_call" | custom-call | flops 1585446912 | bytes 2752512 | tf_op jit(solution)/shard_map/pallas_call | solution.py:461
  64.7 1.3 %shard_map.132 = (bf16[4,1024]{1,0:T(4,128)(2,1)}, bf16[4,1024]{1,0:T(4,128)(2,1)}) custom-call(bf16[4,1024]{1,0:T(4,128)(2,1)} %get-tuple-element.4.old_ref, bf16[4,1024]{1,0:T(4,128)(2,1)} %get-tuple-element.5.new_ref), custom_call_target="tpu_custom_call" | custom-call | tf_op jit(solution)/shard_map/pallas_call | solution.py:473
